TPU v7x, 512 devices: a whole 4x8x8 slice. The times are simulated.
512 devices in a mesh: owner: 32 (over x, z), split: 16 (over y, core).
Axes of the slice: x: 4, y: 8, z: 8, core: 2. Of those that a mesh axis runs over, the one named last changes fastest.
Arguments:
- new_rows: bfloat16 [65536, 256], P(('owner', 'split')), may hold values from -6 to 6
- cluster_ids: int32 [65536], P(('owner', 'split')), may hold values from 0 to 255, as said below
- slot_of_cluster: int32 [256], replicated, may hold values from 0 to 255, as said below
- row_counts: int32 [32, 16, 8], P('owner', 'split'), may hold values from 1 to 1024, 2048 in all within a row
- resident: bfloat16 [32, 16, 2048, 256], P('owner', 'split'), may hold values from -6 to 6
Outputs:
- max_cos: float32 [65536], P(('owner', 'split'))
- centroids: float32 [256, 256], P('owner')
Inputs may be any that keep to these rules, and one draw needn't show every extreme that they name: `slot_of_cluster`: A permutation of the 256 slots. `cluster_ids`: the new rows of one device name clusters of at most 8 rows per owner group; for each index of split, one owner group gets exactly 8 rows from every device of that split index. `row_counts`: each device's counts sum to 2048.
All inputs are finite; a program needn't handle non-finite values.
Results may differ from a plain program's by a relative error of at most 0.0003.
Values may be sent and summed in bfloat16 or wider, within the bound.
A program may use at most 64 MiB of HBM per device.

v0:
```python
import jax
import jax.numpy as jnp
from jax import lax
from jax.sharding import PartitionSpec as P


def scale_rows(values):
    floats = values.astype(jnp.float32)
    return lax.rsqrt(jnp.sum(floats * floats, axis=-1) + 1e-06)


def unit_rows(values):
    return values.astype(jnp.float32) * scale_rows(values)[..., None]


def lookup(indices, small_table):
    match = indices[:, None] == jnp.arange(small_table.shape[0], dtype=jnp.int32)[None, :]
    return jnp.sum(jnp.where(match, small_table[None, :], 0), axis=1)


def best_in_cluster(queries, members, held_rows, inv_held, row_begin, row_end):
    inner = lax.dot_general(
        queries, held_rows, (((1,), (1,)), ((), ())), preferred_element_type=jnp.float32
    )
    inner = inner * inv_held[None, :]
    low = lookup(members, row_begin)
    high = lookup(members, row_end)
    row_index = jnp.arange(held_rows.shape[0], dtype=jnp.int32)[None, :]
    inside = (row_index >= low[:, None]) & (row_index < high[:, None])
    return jnp.max(jnp.where(inside, inner, -3.0), axis=1)


def new_sums(queries, members, clusters):
    weights = (members[None, :] == jnp.arange(clusters, dtype=jnp.int32)[:, None]).astype(
        jnp.float32
    )
    return jnp.dot(weights, unit_rows(queries), precision=lax.Precision.HIGHEST)


def body(new_rows, cluster_ids, slot_of_cluster, row_counts, resident):
    owners = lax.axis_size("owner")
    local_rows = new_rows.shape[0]
    feature_width = new_rows.shape[1]
    clusters = row_counts.shape[2]
    capacity = 2 * local_rows // owners
    split_index = lax.axis_index("split")
    slot_ids = lookup(cluster_ids, slot_of_cluster)
    target = slot_ids // clusters
    member = slot_ids % clusters
    target_hot = (target[:, None] == jnp.arange(owners, dtype=jnp.int32)[None, :]).astype(jnp.int32)
    before = jnp.cumsum(target_hot, axis=0) - target_hot
    position = jnp.sum(before * target_hot, axis=1)
    flat_slot = target * capacity + position
    send_rows = (
        jnp.zeros((owners * capacity, feature_width), jnp.bfloat16).at[flat_slot].set(new_rows)
    )
    send_rows = send_rows.reshape(owners, capacity, feature_width)
    send_member = (
        jnp.full((owners * capacity,), -1, jnp.int32)
        .at[flat_slot]
        .set(member)
        .reshape(owners, capacity)
    )
    held_rows = resident[0, 0]
    counts = row_counts[0, 0]
    row_end = jnp.cumsum(counts)
    row_begin = row_end - counts
    inv_held = scale_rows(held_rows)
    row_cluster = jnp.sum(
        (jnp.arange(held_rows.shape[0], dtype=jnp.int32)[:, None] >= row_end[None, :]).astype(
            jnp.int32
        ),
        axis=1,
    )
    held_weights = (row_cluster[None, :] == jnp.arange(clusters, dtype=jnp.int32)[:, None]).astype(
        jnp.float32
    )
    held_sum = jnp.dot(
        held_weights,
        held_rows.astype(jnp.float32) * inv_held[:, None],
        precision=lax.Precision.HIGHEST,
    )
    arrived, arrived_member = (
        lax.all_to_all(send_rows, "owner", split_axis=0, concat_axis=0, tiled=True),
        lax.all_to_all(send_member, "owner", split_axis=0, concat_axis=0, tiled=True),
    )
    queries = arrived.reshape(-1, feature_width)
    members = arrived_member.reshape(-1)
    share_rows = queries.shape[0]
    piece_rows = lax.all_gather(queries, "split", axis=0, tiled=True)
    piece_members = lax.all_gather(members, "split", axis=0, tiled=True)
    found_max = best_in_cluster(piece_rows, piece_members, held_rows, inv_held, row_begin, row_end)
    best_found = found_max
    best_found = lax.pmax(best_found, "split")
    own_found = lax.dynamic_slice_in_dim(best_found, split_index * share_rows, share_rows, 0)
    own_best = own_found * scale_rows(queries)
    returned = lax.all_to_all(
        own_best.reshape(owners, capacity), "owner", split_axis=0, concat_axis=0, tiled=True
    )
    partial_sum = held_sum + new_sums(queries, members, clusters)
    cluster_total = lax.psum(partial_sum, "split")
    max_cos = returned.reshape(-1)[flat_slot]
    return (max_cos, unit_rows(cluster_total))


def solution(mesh):
    placed = (
        P(("owner", "split"), None),
        P(("owner", "split")),
        P(),
        P("owner", "split", None),
        P("owner", "split", None, None),
    )
    return jax.shard_map(
        body,
        mesh=mesh,
        in_specs=placed,
        out_specs=(P(("owner", "split")), P("owner", None)),
        check_vma=False,
    )
```

profile of v0, /device:TPU:1, one launch (start us, length us, event | category | flops | bytes accessed | tf_op | source)
XLA Modules:
  0.0 174.8 jit_solution(5535262512906054079)
XLA Ops:
  7.2 0.9 select_reduce_fusion.3
  8.6 1.4 scatter_custom_fusion.1
  10.0 22.8 %all_to_all.23 = bf16[32,8,256]{2,1,0:T(8,128)(2,1)} all-to-all(bf16[32,8,256]{2,1,0:T(8,128)(2,1)S(1)} %bitcast.41), channel_id=1, replica_groups=mesh['owner'=32,'split'=16] {'owner'}, dimensions={0} | all-to-all | bytes 262144 | tf_op jit(solution)/shard_map/all_to_all | solution.py:84
  32.8 1.0 scatter_custom_fusion
  33.8 0.7 all_to_all.15
  34.5 3.8 %all-to-all-start = ((s32[32,1,8]{2,1,0:T(1,128)}), s32[32,1,8]{2,1,0:T(1,128)S(1)}, u32[]{:S(2)}, u32[]{:S(2)}) async-start(s32[32,1,8]{2,1,0:T(1,128)} %bitcast.3), calls=%async_computation | async-start | bytes 32768 | tf_op jit(solution)/shard_map/all_to_all | solution.py:85
  38.3 0.8 reduce-window.7
  39.3 1.6 fusion.1
  40.8 0.7 bitcast_subtract_fusion
  41.5 5.4 %all-to-all-done = s32[32,1,8]{2,1,0:T(1,128)S(1)} async-done(((s32[32,1,8]{2,1,0:T(1,128)}), s32[32,1,8]{2,1,0:T(1,128)S(1)}, u32[]{:S(2)}, u32[]{:S(2)}) %all-to-all-start) | async-done | bytes 1056 | tf_op jit(solution)/shard_map/all_to_all | solution.py:85
  47.6 0.7 reduce.9
  48.4 20.6 %all-gather = s32[16,1,256]{2,1,0:T(1,128)S(1)} all-gather(s32[1,1,256]{2,1,0:T(1,128)S(1)} %reshape.185), channel_id=1, replica_groups=mesh['owner'=32,'split'=16] {'split'}, dimensions={0}, use_global_device_ids=true | all-gather | bytes 17408 | tf_op jit(solution)/shard_map/all_gather | solution.py:91
  69.1 1.0 multiply_reduce_fusion
  70.3 1.2 fusion.7
  71.5 1.0 fusion.3
  72.5 23.5 %psum.7 = f32[8,256]{1,0:T(8,128)S(1)} all-reduce(f32[8,256]{1,0:T(8,128)S(1)} %fusion.3), channel_id=1, replica_groups=mesh['owner'=32,'split'=16] {'split'}, use_global_device_ids=true, to_apply=%region_13.14 | all-reduce | flops 2048 | bytes 16384 | tf_op jit(solution)/shard_map/psum | solution.py:101
  96.2 11.9 %select_reduce_fusion = f32[4096]{0:T(1024)S(1)} fusion(f32[2048]{0:T(1024)S(1)} %add_rsqrt_fusion.1, s32[4096]{0:T(1024)S(1)} %get-tuple-element.3, s32[4096]{0:T(1024)S(1)} %get-tuple-element.2, bf16[4096,256]{1,0:T(8,128)(2,1)} %all-gather.3.cloned.1.call-done, bf16[1,1,2048,256]{3,2,1,0:T(8,128)(2,1)S(1)} %copy-done), kind=kOutput, calls=%fused_computation.3 | convolution fusion | flops 4345294848 | bytes 3203072 | tf_op jit(solution)/shard_map/dot_general | solution.py:22
  108.1 43.6 %pmax.7 = f32[4096]{0:T(1024)S(1)} all-reduce(f32[4096]{0:T(1024)S(1)} %select_reduce_fusion), channel_id=1, replica_groups=mesh['owner'=32,'split'=16] {'split'}, use_global_device_ids=true, to_apply=%region_10.11 | all-reduce | flops 4096 | bytes 32768 | tf_op jit(solution)/shard_map/pmax | solution.py:94
  151.7 0.7 all_to_all.18
  152.4 3.9 %all-to-all-start.2 = ((f32[32,1,8]{2,1,0:T(1,128)}), f32[32,1,8]{2,1,0:T(1,128)S(1)}, u32[]{:S(2)}, u32[]{:S(2)}) async-start(f32[32,1,8]{2,1,0:T(1,128)} %bitcast.11), calls=%async_computation.2 | async-start | bytes 32768 | tf_op jit(solution)/shard_map/all_to_all | solution.py:97
  156.3 0.7 broadcast_multiply_fusion
  157.0 7.9 %all-to-all-done.2 = f32[32,1,8]{2,1,0:T(1,128)S(1)} async-done(((f32[32,1,8]{2,1,0:T(1,128)}), f32[32,1,8]{2,1,0:T(1,128)S(1)}, u32[]{:S(2)}, u32[]{:S(2)}) %all-to-all-start.2) | async-done | bytes 1056 | tf_op jit(solution)/shard_map/all_to_all | solution.py:97
  165.4 0.7 reduce.10
  166.2 1.8 %gather_fusion = f32[128]{0:T(128)} fusion(f32[256]{0:T(256)S(1)} %reshape.160, s32[1024]{0:T(1024)S(1)} %pad_clamp_fusion), kind=kCustom, calls=%fused_computation | custom fusion | bytes 1536 | tf_op jit(solution)/shard_map/gather | solution.py:102
  (24 shorter events, 2.4 us)
Async XLA Ops:
  7.2 64.3 %copy-start = (bf16[1,1,2048,256]{3,2,1,0:T(8,128)(2,1)S(1)}, bf16[1,1,2048,256]{3,2,1,0:T(8,128)(2,1)}, u32[]{:S(2)}) copy-start(bf16[1,1,2048,256]{3,2,1,0:T(8,128)(2,1)} %param.9) | copy-start | bytes 3145732
  7.2 89.0 %all-gather.3.cloned.1.call-start = ((), (), s32[]{:S(2)}) async-start(), calls=%async_computation.3 | async-start | bytes 2228224 | tf_op jit(solution)/shard_map/all_gather | solution.py:90
  34.5 12.5 %all-to-all-start = ((s32[32,1,8]{2,1,0:T(1,128)}), s32[32,1,8]{2,1,0:T(1,128)S(1)}, u32[]{:S(2)}, u32[]{:S(2)}) async-start(s32[32,1,8]{2,1,0:T(1,128)} %bitcast.3), calls=%async_computation | async-start | bytes 32768 | tf_op jit(solution)/shard_map/all_to_all | solution.py:85
  152.4 12.5 %all-to-all-start.2 = ((f32[32,1,8]{2,1,0:T(1,128)}), f32[32,1,8]{2,1,0:T(1,128)S(1)}, u32[]{:S(2)}, u32[]{:S(2)}) async-start(f32[32,1,8]{2,1,0:T(1,128)} %bitcast.11), calls=%async_computation.2 | async-start | bytes 32768 | tf_op jit(solution)/shard_map/all_to_all | solution.py:97
Sparse Core Ops, SparseCore 0:
  32.9 38.9 all-gather.2
where the time goes:
time: 178 us; the launch traced here: 175 us
  blocking collectives  111 us (62%)
  between operations  14.2 us (8%)
  matrix products  14.1 us (8%)
  waiting for transfers between devices  13.4 us (8%)
  other arithmetic  7.96 us (4%)
  starting transfers between devices  7.72 us (4%)
  local copies, waits for them, and re-layouts  6.87 us (4%)
    pmax x1, blocking collectives, body(): best_found = lax.pmax(best_found, 'split')  43.6 us
    psum x1, blocking collectives, body(): cluster_total = lax.psum(partial_sum, 'split')  23.5 us
    all_to_all x1, blocking collectives, body(): lax.all_to_all(send_rows, 'owner', split_axis=0, concat_axis=0, tiled=True)  22.8 us
    all_gather x1, blocking collectives, body(): piece_members = lax.all_gather(members, 'split', axis=0, tiled=True)  20.6 us
    dot_general x1, matrix products, best_in_cluster(): lax.dot_general(queries, held_rows, (((1,), (1,)), ((), ())), preferred_e...  11.9 us
    all_to_all x1, waiting for transfers between devices, body(): lax.all_to_all(own_best.reshape(owners, capacity), 'owner', split_axis=0,...  7.95 us
    all_to_all x1, waiting for transfers between devices, body(): lax.all_to_all(send_member, 'owner', split_axis=0, concat_axis=0, tiled=T...  5.45 us
    all_to_all x1, starting transfers between devices, body(): lax.all_to_all(own_best.reshape(owners, capacity), 'owner', split_axis=0,...  3.85 us
  transfers between devices with their start and end apart: 3, of which 2 were waited for; matrix products, arithmetic and copies ran while one was open for 6% of the time, Pallas kernels for 0%

commit v1 on v0

v1 whole, which is shorter than its diff:
```python
import functools

import jax
import jax.numpy as jnp
from jax import lax
from jax.experimental import pallas as pl
from jax.experimental.pallas import tpu as pltpu
from jax.sharding import PartitionSpec as P

F32, BF16, I32 = jnp.float32, jnp.bfloat16, jnp.int32
MESH = pl.DeviceIdType.MESH
NT = (((1,), (1,)), ((), ()))
NN = (((1,), (0,)), ((), ()))
EPS = 1e-06
LOWEST = -3.0


def iota(shape, dim):
    return lax.broadcasted_iota(I32, shape, dim)


def mm(lhs, rhs, dims=NN):
    return lax.dot_general(lhs, rhs, dims, preferred_element_type=F32)


def column_to_row(column):
    pieces = []
    for start in range(0, column.shape[0], 128):
        piece = column[start : start + 128]
        n = piece.shape[0]
        wide = jnp.broadcast_to(piece, (n, n))
        eye = iota((n, n), 0) == iota((n, n), 1)
        pieces.append(jnp.sum(jnp.where(eye, wide, 0.0), axis=0, keepdims=True))
    return pieces[0] if len(pieces) == 1 else jnp.concatenate(pieces, axis=1)


def split_weights(mask, row):
    high = row.astype(BF16).astype(F32)
    low = row - high
    return jnp.concatenate(
        [jnp.where(mask, high, 0.0), jnp.where(mask, low, 0.0)], axis=0
    ).astype(BF16)


def kernel(
    dims,
    ids_ref,
    table_ref,
    counts_ref,
    rows_ref,
    resident_ref,
    max_ref,
    cent_ref,
    held,
    scale_col,
    cluster_col,
    send_rows,
    send_members,
    got_rows,
    got_members,
    blocks,
    members,
    part,
    part_got,
    total_own,
    total,
    best_own,
    best_got,
    ret_own,
    ret_got,
    load_sem,
    sems,
    major_send,
    major_recv,
    minor_send,
    minor_recv,
    sib_send,
    sib_recv,
):
    owners, splits, local, width, clusters, res_rows, cap = dims
    slots = owners * cap
    half = slots // 2
    lane_group = min(128, slots)
    groups = slots // lane_group
    owners_in_group = lane_group // cap
    chunk = clusters * width // splits
    chunks_in_row = width // chunk
    ny = splits // 2
    me_o = lax.axis_index("owner")
    me_s = lax.axis_index("split")
    y = me_s // 2
    core = me_s - 2 * y
    step_dir = 1 - 2 * core
    sibling = 2 * y + 1 - core

    def at_y(offset):
        return 2 * lax.rem(y + offset * step_dir + 4 * ny, ny) + core

    def sib_at_y(offset):
        return 2 * lax.rem(y - offset * step_dir + 4 * ny, ny) + 1 - core

    def other_owner(k):
        return lax.rem(me_o + k, owners)

    def other_split(k):
        return lax.rem(me_s + k, splits)

    def remote(src, dst, send, recv, owner, split):
        return pltpu.make_async_remote_copy(
            src_ref=src,
            dst_ref=dst,
            send_sem=send,
            recv_sem=recv,
            device_id=(owner, split),
            device_id_type=MESH,
        )

    def wait_all(ref, count, kind, side):
        piece = ref.at[pl.ds(0, count)]
        pltpu.make_async_copy(piece, piece, sems.at[kind, side]).wait()

    ROWS, MEMBERS, GATHER, PART, TOTAL, BEST, RET = range(7)

    load = pltpu.make_async_copy(resident_ref, held, load_sem)
    load.start()

    barrier = pltpu.get_barrier_semaphore()

    @pl.loop(1, owners)
    def _(k):
        pl.semaphore_signal(
            barrier, inc=1, device_id=(other_owner(k), me_s), device_id_type=MESH
        )

    @pl.loop(1, splits)
    def _(k):
        pl.semaphore_signal(
            barrier, inc=1, device_id=(me_o, other_split(k)), device_id_type=MESH
        )

    ids = ids_ref[...]
    count_of_clusters = table_ref.shape[1]
    hot = jnp.where(iota((count_of_clusters, local), 0) == ids, 1.0, 0.0).astype(BF16)
    table = jnp.broadcast_to(table_ref[...].astype(F32), (8, count_of_clusters)).astype(BF16)
    slot = mm(table, hot)[0:1].astype(I32)
    target = lax.div(slot, clusters)
    member = slot - target * clusters
    target_hot = jnp.where(iota((owners, local), 0) == target, 1.0, 0.0)
    earlier = jnp.where(iota((local, local), 0) < iota((local, local), 1), 1.0, 0.0).astype(BF16)
    before = mm(target_hot.astype(BF16), earlier)
    place = jnp.sum(target_hot * before, axis=0, keepdims=True).astype(I32)
    flat = target * cap + place
    rows = rows_ref[...]
    scatter = jnp.where(iota((slots, local), 0) == flat, 1.0, 0.0).astype(BF16)
    send_rows[...] = mm(scatter, rows).reshape(owners, cap, width).astype(BF16)
    target_member = (target_hot * (member + 1).astype(F32)).astype(BF16)
    place_hot = jnp.where(
        lax.rem(iota((lane_group, local), 0), cap) == place, 1.0, 0.0
    ).astype(BF16)
    member_rows = mm(target_member, place_hot, NT)
    for o in range(owners):
        send_members[o] = member_rows[o : o + 1]

    pl.semaphore_wait(barrier, owners + splits - 2)

    @pl.loop(1, owners)
    def _(k):
        o = other_owner(k)
        remote(
            send_members.at[o],
            got_members.at[me_o],
            sems.at[MEMBERS, 0],
            sems.at[MEMBERS, 1],
            o,
            me_s,
        ).start()
        remote(
            send_rows.at[o],
            got_rows.at[me_o],
            sems.at[ROWS, 0],
            sems.at[ROWS, 1],
            o,
            me_s,
        ).start()

    got_rows[me_o] = send_rows[me_o]
    got_members[me_o] = send_members[me_o]

    floats = rows.astype(F32)
    own_scale = lax.rsqrt(
        column_to_row(jnp.sum(floats * floats, axis=1, keepdims=True)) + EPS
    )
    ends = []
    running = counts_ref[0, 0]
    for j in range(clusters):
        ends.append(running)
        if j + 1 < clusters:
            running = running + counts_ref[0, j + 1]
    load.wait()
    step_rows = 256

    def cluster_of(index):
        result = jnp.ones(index.shape, I32)
        for end in ends[:-1]:
            result = result + jnp.where(index >= end, 1, 0)
        return result

    def held_step(t, acc):
        start = pl.multiple_of(t * step_rows, step_rows)
        x = held[pl.ds(start, step_rows)]
        f = x.astype(F32)
        scale = lax.rsqrt(jnp.sum(f * f, axis=1, keepdims=True) + EPS)
        scale_col[pl.ds(start, step_rows)] = jnp.broadcast_to(scale, (step_rows, 128))
        cluster_col[pl.ds(start, step_rows)] = cluster_of(
            iota((step_rows, 128), 0) + start
        ).astype(F32)
        row = column_to_row(scale)
        mask = cluster_of(iota((clusters, step_rows), 1) + start) == iota(
            (clusters, step_rows), 0
        ) + 1
        return acc + mm(split_weights(mask, row), x)

    held_sum = lax.fori_loop(
        0, res_rows // step_rows, held_step, jnp.zeros((2 * clusters, width), F32)
    )

    wait_all(got_members, owners - 1, MEMBERS, 1)
    pieces = []
    for g in range(groups):
        owner_of_lane = lax.div(iota((1, lane_group), 1), cap) + g * owners_in_group
        acc = jnp.zeros((1, lane_group), F32)
        for o in range(g * owners_in_group, (g + 1) * owners_in_group):
            acc = acc + jnp.where(owner_of_lane == o, got_members[o], 0.0)
        pieces.append(acc)
    own_members = pieces[0] if groups == 1 else jnp.concatenate(pieces, axis=1)
    members[me_s] = own_members

    @pl.loop(1, splits)
    def _(k):
        s = other_split(k)
        remote(
            members.at[me_s],
            members.at[me_s],
            sems.at[GATHER, 0],
            sems.at[GATHER, 1],
            me_o,
            s,
        ).start()

    wait_all(got_rows, owners - 1, ROWS, 1)
    own_block = got_rows[...].astype(F32).reshape(slots, width)
    for h in range(2):
        blocks[2 * me_s + h] = own_block[h * half : (h + 1) * half].astype(BF16)

    last_major, last_minor = ny // 2, ny // 2 - 1
    up, down = at_y(1), at_y(-1)

    def major(k, h):
        slot_ref = blocks.at[2 * at_y(1 - k) + h]
        return remote(slot_ref, slot_ref, major_send.at[k - 1, h], major_recv.at[k - 1, h], me_o, up)

    def minor(k, h):
        slot_ref = blocks.at[2 * at_y(k - 1) + h]
        return remote(slot_ref, slot_ref, minor_send.at[k - 1, h], minor_recv.at[k - 1, h], me_o, down)

    def to_sibling(index, offset, h):
        slot_ref = blocks.at[2 * at_y(offset) + h]
        return remote(slot_ref, slot_ref, sib_send.at[index, h], sib_recv.at[index, h], me_o, sibling)

    def major_arrived(k, h):
        slot_ref = blocks.at[2 * at_y(-k) + h]
        remote(slot_ref, slot_ref, major_send.at[k - 1, h], major_recv.at[k - 1, h], me_o, up).wait_recv()

    def minor_arrived(k, h):
        slot_ref = blocks.at[2 * at_y(k) + h]
        remote(slot_ref, slot_ref, minor_send.at[k - 1, h], minor_recv.at[k - 1, h], me_o, down).wait_recv()

    def sibling_arrived(index, offset):
        for h in range(2):
            slot_ref = blocks.at[2 * sib_at_y(offset) + h]
            remote(
                slot_ref, slot_ref, sib_send.at[index, h], sib_recv.at[index, h], me_o, sibling
            ).wait_recv()

    for h in range(2):
        if last_major:
            major(1, h).start()
        if last_minor:
            minor(1, h).start()
        to_sibling(0, 0, h).start()

    def score(s):
        queries = blocks[pl.ds(2 * s, 2)].reshape(slots, width)
        wanted = members[s]
        score_rows = min(512, res_rows)

        def step(t, best):
            start = pl.multiple_of(t * score_rows, score_rows)
            inner = mm(held[pl.ds(start, score_rows)], queries, NT)
            kept = []
            for g in range(groups):
                lanes = slice(g * lane_group, (g + 1) * lane_group)
                value = inner[:, lanes] * scale_col[pl.ds(start, score_rows)][:, :lane_group]
                inside = cluster_col[pl.ds(start, score_rows)][:, :lane_group] == wanted[:, lanes]
                value = jnp.where(inside, value, LOWEST)
                kept.append(jnp.max(value.reshape(score_rows // 8, 8, lane_group), axis=0))
            new = kept[0] if groups == 1 else jnp.concatenate(kept, axis=1)
            return jnp.maximum(best, new)

        best = lax.fori_loop(
            0, res_rows // score_rows, step, jnp.full((8, slots), LOWEST, F32)
        )
        return jnp.max(best, axis=0, keepdims=True)

    def score_and_send(s):
        best_own[s] = score(s)
        remote(
            best_own.at[s],
            best_got.at[me_s],
            sems.at[BEST, 0],
            sems.at[BEST, 1],
            me_o,
            s,
        ).start()

    block_scale = lax.rsqrt(
        column_to_row(jnp.sum(own_block * own_block, axis=1, keepdims=True)) + EPS
    )
    new_mask = jnp.broadcast_to(own_members, (clusters, slots)) == (
        iota((clusters, slots), 0) + 1
    ).astype(F32)
    both = held_sum + mm(split_weights(new_mask, block_scale), own_block.astype(BF16))
    partial = both[:clusters] + both[clusters:]
    for s in range(splits):
        row, lane = s // chunks_in_row, (s % chunks_in_row) * chunk
        part[s] = partial[row : row + 1, lane : lane + chunk]

    @pl.loop(1, splits)
    def _(k):
        s = other_split(k)
        remote(
            part.at[s], part_got.at[me_s], sems.at[PART, 0], sems.at[PART, 1], me_o, s
        ).start()

    part_got[me_s] = part[me_s]

    wait_all(members, splits - 1, GATHER, 1)
    best_got[me_s] = score(me_s)

    for k in range(1, last_major + 1):
        for h in range(2):
            major_arrived(k, h)
            if k < last_major:
                major(k + 1, h).start()
            to_sibling(k, -k, h).start()
            if k <= last_minor:
                minor_arrived(k, h)
                if k < last_minor:
                    minor(k + 1, h).start()
                to_sibling(last_major + k, k, h).start()
            if h == 0:
                if k == 1:
                    sibling_arrived(0, 0)
                    score_and_send(sib_at_y(0))
                else:
                    sibling_arrived(k - 1, -(k - 1))
                    score_and_send(sib_at_y(-(k - 1)))
                    sibling_arrived(last_major + k - 1, k - 1)
                    score_and_send(sib_at_y(k - 1))
        score_and_send(at_y(-k))
        if k <= last_minor:
            score_and_send(at_y(k))
        if k == 1:
            wait_all(part_got, splits - 1, PART, 1)
            total_own[...] = jnp.sum(part_got[...], axis=0)

            @pl.loop(1, splits)
            def _(j):
                remote(
                    total_own, total.at[me_s], sems.at[TOTAL, 0], sems.at[TOTAL, 1], me_o, other_split(j)
                ).start()

            total[me_s] = total_own[...]
    sibling_arrived(last_major, -last_major)
    score_and_send(sib_at_y(-last_major))

    wait_all(total, splits - 1, TOTAL, 1)
    summed = []
    for j in range(clusters):
        bits = [total[j * chunks_in_row + i] for i in range(chunks_in_row)]
        summed.append(bits[0] if chunks_in_row == 1 else jnp.concatenate(bits, axis=1))
    for j in range(clusters):
        v = summed[j]
        cent_ref[j : j + 1] = v * lax.rsqrt(jnp.sum(v * v, axis=1, keepdims=True) + EPS)

    wait_all(best_got, splits - 1, BEST, 1)
    best = jnp.max(best_got[...], axis=0)
    for g in range(groups):
        ret_own[g] = best[:, g * lane_group : (g + 1) * lane_group]

    @pl.loop(1, owners)
    def _(k):
        o = other_owner(k)
        remote(
            ret_own.at[lax.div(o, owners_in_group)],
            ret_got.at[me_o],
            sems.at[RET, 0],
            sems.at[RET, 1],
            o,
            me_s,
        ).start()

    ret_got[me_o] = ret_own[lax.div(me_o, owners_in_group)]

    wait_all(send_rows, owners - 1, ROWS, 0)
    wait_all(send_members, owners - 1, MEMBERS, 0)
    wait_all(members, splits - 1, GATHER, 0)
    wait_all(part, splits - 1, PART, 0)
    wait_all(total, splits - 1, TOTAL, 0)
    wait_all(best_own, splits - 1, BEST, 0)
    for h in range(2):
        for k in range(1, last_major + 1):
            major(k, h).wait_send()
            to_sibling(k, -k, h).wait_send()
        for k in range(1, last_minor + 1):
            minor(k, h).wait_send()
            to_sibling(last_major + k, k, h).wait_send()
        to_sibling(0, 0, h).wait_send()

    wait_all(ret_got, owners - 1, RET, 1)
    lane_of_row = lax.rem(me_o, owners_in_group) * cap + place
    lane_hot = iota((lane_group, local), 0) == lane_of_row
    table_rows = jnp.concatenate([ret_got[o] for o in range(owners)], axis=0)
    high = table_rows.astype(BF16).astype(F32)
    mid = (table_rows - high).astype(BF16).astype(F32)
    low = table_rows - high - mid
    stacked = jnp.concatenate([high, mid, low], axis=0).astype(BF16)
    picked = mm(stacked, jnp.where(lane_hot, 1.0, 0.0).astype(BF16))
    picked = picked[:owners] + picked[owners : 2 * owners] + picked[2 * owners :]
    max_ref[...] = own_scale * jnp.sum(target_hot * picked, axis=0, keepdims=True)
    wait_all(ret_got, owners - 1, RET, 0)


def body(new_rows, cluster_ids, slot_of_cluster, row_counts, resident):
    owners, splits = lax.axis_size("owner"), lax.axis_size("split")
    local, width = new_rows.shape
    clusters = row_counts.shape[2]
    res_rows = resident.shape[2]
    cap = 2 * local // owners
    slots = owners * cap
    half = slots // 2
    lane_group = min(128, slots)
    chunk = clusters * width // splits
    ny = splits // 2
    vmem = pl.BlockSpec(memory_space=pltpu.VMEM)
    dma = pltpu.SemaphoreType.DMA
    best, centroids = pl.pallas_call(
        functools.partial(kernel, (owners, splits, local, width, clusters, res_rows, cap)),
        out_shape=(
            jax.ShapeDtypeStruct((1, local), F32),
            jax.ShapeDtypeStruct((clusters, width), F32),
        ),
        in_specs=[
            vmem,
            vmem,
            pl.BlockSpec(memory_space=pltpu.SMEM),
            vmem,
            pl.BlockSpec(memory_space=pl.ANY),
        ],
        out_specs=(vmem, vmem),
        scratch_shapes=[
            pltpu.VMEM((res_rows, width), BF16),
            pltpu.VMEM((res_rows, 128), F32),
            pltpu.VMEM((res_rows, 128), F32),
            pltpu.VMEM((owners, cap, width), BF16),
            pltpu.VMEM((owners, 1, lane_group), F32),
            pltpu.VMEM((owners, cap, width), BF16),
            pltpu.VMEM((owners, 1, lane_group), F32),
            pltpu.VMEM((2 * splits, half, width), BF16),
            pltpu.VMEM((splits, 1, slots), F32),
            pltpu.VMEM((splits, 1, chunk), F32),
            pltpu.VMEM((splits, 1, chunk), F32),
            pltpu.VMEM((1, chunk), F32),
            pltpu.VMEM((splits, 1, chunk), F32),
            pltpu.VMEM((splits, 1, slots), F32),
            pltpu.VMEM((splits, 1, slots), F32),
            pltpu.VMEM((slots // lane_group, 1, lane_group), F32),
            pltpu.VMEM((owners, 1, lane_group), F32),
            dma,
            dma((7, 2)),
            dma((max(1, ny // 2), 2)),
            dma((max(1, ny // 2), 2)),
            dma((max(1, ny // 2 - 1), 2)),
            dma((max(1, ny // 2 - 1), 2)),
            dma((ny, 2)),
            dma((ny, 2)),
        ],
        compiler_params=pltpu.CompilerParams(
            collective_id=0, has_side_effects=True, vmem_limit_bytes=48 * 1024 * 1024
        ),
        cost_estimate=pl.CostEstimate(
            flops=2 * splits * slots * res_rows * width, bytes_accessed=4 << 20, transcendentals=0
        ),
    )(
        cluster_ids.reshape(1, -1),
        slot_of_cluster.reshape(1, -1),
        row_counts.reshape(1, -1),
        new_rows,
        resident.reshape(res_rows, width),
    )
    return best.reshape(-1), centroids


def solution(mesh):
    placed = (
        P(("owner", "split"), None),
        P(("owner", "split")),
        P(),
        P("owner", "split", None),
        P("owner", "split", None, None),
    )
    return jax.shard_map(
        body,
        mesh=mesh,
        in_specs=placed,
        out_specs=(P(("owner", "split")), P("owner", None)),
        check_vma=False,
    )
```

time: 178 us -> 61.4 us (0.34); the launches traced: 175 us -> 61.2 us
  blocking collectives: 111 us -> 0 us
  Pallas kernels: 0 us -> 56.6 us
  matrix products: 14.1 us -> 0 us
  between operations: 14.2 us -> 0.67 us
  waiting for transfers between devices: 13.4 us -> 0 us
  other arithmetic: 7.96 us -> 0 us
  starting transfers between devices: 7.72 us -> 0 us
  local copies, waits for them, and re-layouts: 6.87 us -> 3.85 us
    pallas_call x0 -> x1, Pallas kernels: none -> 56.6 us  [body(): pl.pallas_call(functools.partial(kernel, (owners, splits, local, width, c...]
    pmax x1 -> x0, blocking collectives: 43.6 us -> none  [body(): best_found = lax.pmax(best_found, 'split')]
    psum x1 -> x0, blocking collectives: 23.5 us -> none  [body(): cluster_total = lax.psum(partial_sum, 'split')]
    all_to_all x1 -> x0, blocking collectives: 22.8 us -> none  [body(): lax.all_to_all(send_rows, 'owner', split_axis=0, concat_axis=0, tiled=True)]
    all_gather x1 -> x0, blocking collectives: 20.6 us -> none  [body(): piece_members = lax.all_gather(members, 'split', axis=0, tiled=True)]
    dot_general x3 -> x0, matrix products: 14.1 us -> none  [the longest x1 11.9 us: best_in_cluster(): lax.dot_general(queries, held_rows, (((1,), (1,)), ((), ())), preferred_e...]
    all_to_all x2 -> x0, waiting for transfers between devices: 13.4 us -> none  [the longest x1 7.95 us: body(): lax.all_to_all(own_best.reshape(owners, capacity), 'owner', split_axis=0,...]
    all_to_all x2 -> x0, starting transfers between devices: 7.68 us -> none  [the longest x1 3.85 us: body(): lax.all_to_all(own_best.reshape(owners, capacity), 'owner', split_axis=0,...]
  transfers between devices with their start and end apart: 3 -> 0, of which waited for: 2 -> 0; matrix products, arithmetic and copies ran while one was open for 6% -> 0% of each run, Pallas kernels for 0% -> 0%
where the time goes in v1:
time: 61.4 us; the launch traced here: 61.2 us
  Pallas kernels  56.6 us (92%)
  local copies, waits for them, and re-layouts  3.85 us (6%)
  between operations  0.67 us (1%)
    pallas_call x1, Pallas kernels, body(): pl.pallas_call(functools.partial(kernel, (owners, splits, local, width, c...  56.6 us
    unnamed x12, local copies, waits for them, and re-layouts  3.85 us

profile of v1, /device:TPU:1, one launch (start us, length us, event | category | flops | bytes accessed | tf_op | source)
XLA Modules:
  0.0 61.2 jit_solution(2115456082873816044)
XLA Ops:
  0.6 0.0 copy-start.4
  0.6 0.0 copy-start.2
  0.7 0.0 copy-start.3
  0.7 0.6 %copy-done.4 = s32[1,1,8]{2,1,0:T(1,128)S(1)} copy-done((s32[1,1,8]{2,1,0:T(1,128)S(1)}, s32[1,1,8]{2,1,0:T(1,128)}, u32[]{:S(2)}) %copy-start.4) | copy-done | bytes 56
  1.3 0.0 copy-done.2
  1.3 0.0 copy-done.3
  1.3 0.0 copy-start
  1.3 1.2 %copy-done = bf16[1,1,2048,256]{3,2,1,0:T(8,128)(2,1)S(1)} copy-done((bf16[1,1,2048,256]{3,2,1,0:T(8,128)(2,1)S(1)}, bf16[1,1,2048,256]{3,2,1,0:T(8,128)(2,1)}, u32[]{:S(2)}) %copy-start) | copy-done | bytes 1048600
  2.6 0.0 copy-start.1
  2.6 0.8 %copy-done.1 = bf16[128,256]{1,0:T(8,128)(2,1)S(1)} copy-done((bf16[128,256]{1,0:T(8,128)(2,1)S(1)}, bf16[128,256]{1,0:T(8,128)(2,1)}, u32[]{:S(2)}) %copy-start.1) | copy-done | bytes 65560
  3.4 56.6 %shard_map.68 = (f32[1,128]{1,0:T(1,128)S(1)}, f32[8,256]{1,0:T(8,128)S(1)}) custom-call(s32[1,128]{1,0:T(1,128)S(1)} %bitcast.7, s32[1,256]{1,0:T(1,128)S(1)} %bitcast.6, s32[1,8]{1,0:T(1,128)S(1)} %bitcast.8, bf16[128,256]{1,0:T(8,128)(2,1)S(1)} %copy-done.1, bf16[2048,256]{1,0:T(8,128)(2,1)S(1)} %bitcast.5), custom_call_target="tpu_custom_call" | custom-call | flops 4294967296 | bytes 4194304 | tf_op jit(solution)/shard_map/pallas_call | solution.py:457
  60.1 0.5 copy.9
  60.6 0.6 copy.10
Async XLA Ops:
  0.6 0.7 %copy-start.4 = (s32[1,1,8]{2,1,0:T(1,128)S(1)}, s32[1,1,8]{2,1,0:T(1,128)}, u32[]{:S(2)}) copy-start(s32[1,1,8]{2,1,0:T(1,128)} %param.8) | copy-start | bytes 100
  0.6 0.7 %copy-start.2 = (s32[256]{0:T(256)S(1)}, s32[256]{0:T(256)}, u32[]{:S(2)}) copy-start(s32[256]{0:T(256)} %param.7) | copy-start | bytes 3076
  0.7 0.7 %copy-start.3 = (s32[128]{0:T(128)S(1)}, s32[128]{0:T(128)}, u32[]{:S(2)}) copy-start(s32[128]{0:T(128)} %param.6) | copy-start | bytes 1540
  1.3 1.2 %copy-start = (bf16[1,1,2048,256]{3,2,1,0:T(8,128)(2,1)S(1)}, bf16[1,1,2048,256]{3,2,1,0:T(8,128)(2,1)}, u32[]{:S(2)}) copy-start(bf16[1,1,2048,256]{3,2,1,0:T(8,128)(2,1)} %param.9) | copy-start | bytes 3145732
  2.6 0.8 %copy-start.1 = (bf16[128,256]{1,0:T(8,128)(2,1)S(1)}, bf16[128,256]{1,0:T(8,128)(2,1)}, u32[]{:S(2)}) copy-start(bf16[128,256]{1,0:T(8,128)(2,1)} %rows_ref.1) | copy-start | bytes 196612

commit v2 on v1

v2 whole, which is shorter than its diff:
```python
import functools

import jax
import jax.numpy as jnp
from jax import lax
from jax.experimental import pallas as pl
from jax.experimental.pallas import tpu as pltpu
from jax.sharding import PartitionSpec as P

F32, BF16, I32 = jnp.float32, jnp.bfloat16, jnp.int32
MESH = pl.DeviceIdType.MESH
NT = (((1,), (1,)), ((), ()))
NN = (((1,), (0,)), ((), ()))
EPS = 1e-06
LOWEST = -3.0
PIECES = 4


def iota(shape, dim):
    return lax.broadcasted_iota(I32, shape, dim)


def mm(lhs, rhs, dims=NN):
    return lax.dot_general(lhs, rhs, dims, preferred_element_type=F32)


def column_to_row(column):
    pieces = []
    for start in range(0, column.shape[0], 128):
        piece = column[start : start + 128]
        n = piece.shape[0]
        wide = jnp.broadcast_to(piece, (n, n))
        eye = iota((n, n), 0) == iota((n, n), 1)
        pieces.append(jnp.sum(jnp.where(eye, wide, 0.0), axis=0, keepdims=True))
    return pieces[0] if len(pieces) == 1 else jnp.concatenate(pieces, axis=1)


def split_weights(mask, row):
    high = row.astype(BF16).astype(F32)
    low = row - high
    return jnp.concatenate(
        [jnp.where(mask, high, 0.0), jnp.where(mask, low, 0.0)], axis=0
    ).astype(BF16)


def displacements(owners):
    across = 4 if owners == 32 else 1
    along = owners // across

    def hops(d):
        return min(d[0], across - d[0]) + min(d[1], along - d[1])

    near = sorted(((dx, dz) for dx in range(across) for dz in range(along)), key=hops)
    return across, along, near


def kernel(
    dims,
    ids_hbm,
    table_hbm,
    counts_hbm,
    rows_hbm,
    resident_hbm,
    max_ref,
    cent_ref,
    ids_ref,
    table_ref,
    counts_ref,
    rows_ref,
    held,
    scale_col,
    cluster_col,
    send_rows,
    send_members,
    got_rows,
    got_members,
    blocks,
    members,
    held_sums,
    part,
    part_got,
    total_own,
    total,
    best_own,
    best_got,
    ret_own,
    ret_got,
    load_sems,
    piece_sems,
    sems,
    major_send,
    major_recv,
    minor_send,
    minor_recv,
    sib_send,
    sib_recv,
):
    owners, splits, local, width, clusters, res_rows, cap = dims
    across, along, near = displacements(owners)
    slots = owners * cap
    lane_group = min(128, slots)
    groups = slots // lane_group
    owners_in_group = lane_group // cap
    piece_owners = owners // PIECES
    piece_rows = slots // PIECES
    chunk = clusters * width // splits
    chunks_in_row = width // chunk
    ny = splits // 2
    last_major, last_minor = ny // 2, ny // 2 - 1
    me_o = lax.axis_index("owner")
    me_s = lax.axis_index("split")
    me_x, me_z = me_o // along, me_o % along
    y = me_s // 2
    core = me_s - 2 * y
    step_dir = 1 - 2 * core
    sibling = 2 * y + 1 - core

    def at_y(offset):
        return 2 * ((y + offset * step_dir + 4 * ny) % ny) + core

    def target_of(r):
        dx, dz = near[r]
        return ((me_x + across - dx) % across) * along + (me_z + along - dz) % along

    def source_of(r):
        dx, dz = near[r]
        return ((me_x + dx) % across) * along + (me_z + dz) % along

    def other_split(k):
        return (me_s + k) % splits

    def remote(src, dst, send, recv, owner, split):
        return pltpu.make_async_remote_copy(
            src_ref=src,
            dst_ref=dst,
            send_sem=send,
            recv_sem=recv,
            device_id=(owner, split),
            device_id_type=MESH,
        )

    def wait_piece(piece, sem):
        pltpu.make_async_copy(piece, piece, sem).wait()

    def wait_all(ref, count, kind, side):
        wait_piece(ref.at[pl.ds(0, count)], sems.at[kind, side])

    ROWS, MEMBERS, PART, TOTAL, BEST, RET = range(6)

    loads = [
        pltpu.make_async_copy(src, dst, load_sems.at[i])
        for i, (src, dst) in enumerate(
            (
                (ids_hbm, ids_ref),
                (table_hbm, table_ref),
                (rows_hbm, rows_ref),
                (counts_hbm, counts_ref),
                (resident_hbm, held),
            )
        )
    ]
    barrier = pltpu.get_barrier_semaphore()

    @pl.loop(1, owners)
    def _(k):
        pl.semaphore_signal(
            barrier, inc=1, device_id=((me_o + k) % owners, me_s), device_id_type=MESH
        )

    for load in loads:
        load.start()

    @pl.loop(1, splits)
    def _(k):
        pl.semaphore_signal(
            barrier, inc=1, device_id=(me_o, other_split(k)), device_id_type=MESH
        )

    loads[0].wait()
    loads[1].wait()
    ids = ids_ref[...]
    all_clusters = table_ref.shape[1]
    hot = jnp.where(iota((all_clusters, local), 0) == ids, 1.0, 0.0).astype(BF16)
    table = jnp.broadcast_to(table_ref[...].astype(F32), (8, all_clusters)).astype(BF16)
    slot = mm(table, hot)[0:1].astype(I32)
    target = lax.div(slot, clusters)
    member = slot - target * clusters
    order = iota((owners, local), 0)
    target_of_order = jnp.zeros((owners, local), I32)
    for r in range(owners):
        target_of_order = jnp.where(order == r, target_of(r), target_of_order)
    target_hot = jnp.where(target_of_order == target, 1.0, 0.0)
    rank = jnp.sum(target_hot * order.astype(F32), axis=0, keepdims=True).astype(I32)
    earlier = jnp.where(iota((local, local), 0) < iota((local, local), 1), 1.0, 0.0).astype(BF16)
    before = mm(target_hot.astype(BF16), earlier)
    place = jnp.sum(target_hot * before, axis=0, keepdims=True).astype(I32)
    flat = rank * cap + place
    target_member = (target_hot * (member + 1).astype(F32)).astype(BF16)
    place_hot = jnp.where(
        lax.rem(iota((lane_group, local), 0), cap) == place, 1.0, 0.0
    ).astype(BF16)
    member_rows = mm(target_member, place_hot, NT)
    for r in range(owners):
        send_members[r] = member_rows[r : r + 1]
    loads[2].wait()
    rows = rows_ref[...]
    scatter = jnp.where(iota((slots, local), 0) == flat, 1.0, 0.0).astype(BF16)
    send_rows[...] = mm(scatter, rows).reshape(owners, cap, width).astype(BF16)

    pl.semaphore_wait(barrier, owners + splits - 2)

    for r in range(owners - 1, 0, -1):
        remote(
            send_rows.at[r],
            got_rows.at[r],
            sems.at[ROWS, 0],
            piece_sems.at[r // piece_owners],
            target_of(r),
            me_s,
        ).start()
        remote(
            send_members.at[r],
            got_members.at[r],
            sems.at[MEMBERS, 0],
            sems.at[MEMBERS, 1],
            target_of(r),
            me_s,
        ).start()
    got_rows[0] = send_rows[0]
    got_members[0] = send_members[0]

    floats = rows.astype(F32)
    own_scale = lax.rsqrt(
        column_to_row(jnp.sum(floats * floats, axis=1, keepdims=True)) + EPS
    )
    loads[3].wait()
    loads[4].wait()
    ends = []
    running = counts_ref[0, 0]
    for j in range(clusters):
        ends.append(running)
        if j + 1 < clusters:
            running = running + counts_ref[0, j + 1]
    step_rows = 256

    def cluster_of(index):
        result = jnp.ones(index.shape, I32)
        for end in ends[:-1]:
            result = result + jnp.where(index >= end, 1, 0)
        return result

    def held_step(t, acc):
        start = pl.multiple_of(t * step_rows, step_rows)
        x = held[pl.ds(start, step_rows)]
        f = x.astype(F32)
        scale = lax.rsqrt(jnp.sum(f * f, axis=1, keepdims=True) + EPS)
        scale_col[pl.ds(start, step_rows)] = jnp.broadcast_to(scale, (step_rows, 128))
        cluster_col[pl.ds(start, step_rows)] = cluster_of(
            iota((step_rows, 128), 0) + start
        ).astype(F32)
        row = column_to_row(scale)
        mask = cluster_of(iota((clusters, step_rows), 1) + start) == iota(
            (clusters, step_rows), 0
        ) + 1
        return acc + mm(split_weights(mask, row), x)

    held_sums[...] = lax.fori_loop(
        0, res_rows // step_rows, held_step, jnp.zeros((2 * clusters, width), F32)
    )

    def piece_of(block, p):
        return members.at[block] if p == PIECES else blocks.at[PIECES * block + p]

    def up(block, k, p, hops=1):
        ref = piece_of(block, p)
        return remote(ref, ref, major_send.at[k - 1, p], major_recv.at[k - 1, p], me_o, at_y(hops))

    def down(block, k, p):
        ref = piece_of(block, p)
        return remote(ref, ref, minor_send.at[k - 1, p], minor_recv.at[k - 1, p], me_o, at_y(-1))

    def aside(block, index, p):
        ref = piece_of(block, p)
        return remote(ref, ref, sib_send.at[index, p], sib_recv.at[index, p], me_o, sibling)

    skip = ny == 8

    def skipped(p):
        return skip and p >= PIECES - 1

    def start_own(p):
        up(me_s, 1, p).start()
        if last_minor:
            down(me_s, 1, p).start()
        aside(me_s, 0, p).start()

    for p in range(PIECES):
        first = max(1, p * piece_owners)
        count = (p + 1) * piece_owners - first
        if count:
            wait_piece(got_rows.at[pl.ds(first, count)], piece_sems.at[p])
        blocks[PIECES * me_s + p] = (
            got_rows[pl.ds(p * piece_owners, piece_owners)]
            .astype(F32)
            .reshape(piece_rows, width)
            .astype(BF16)
        )
        start_own(p)
    wait_all(got_members, owners - 1, MEMBERS, 1)
    pieces = []
    for g in range(groups):
        order_of_lane = lax.div(iota((1, lane_group), 1), cap) + g * owners_in_group
        acc = jnp.zeros((1, lane_group), F32)
        for r in range(g * owners_in_group, (g + 1) * owners_in_group):
            acc = acc + jnp.where(order_of_lane == r, got_members[r], 0.0)
        pieces.append(acc)
    members[me_s] = pieces[0] if groups == 1 else jnp.concatenate(pieces, axis=1)
    start_own(PIECES)

    def handle(k, p):
        block = at_y(-k)
        up(block, k, p).wait_recv()
        if not skipped(p):

            @pl.when(k < last_major)
            def _():
                up(block, k + 1, p).start()

        else:

            @pl.when(k < 3)
            def _():
                up(block, k + 1, p).start()

            @pl.when(k == 2)
            def _():
                up(block, 4, p, hops=2).start()

        aside(block, 2 * k - 1, p).start()
        if last_minor:

            @pl.when(k <= last_minor)
            def _():
                block = at_y(k)
                down(block, k, p).wait_recv()

                @pl.when(k < last_minor)
                def _():
                    down(block, k + 1, p).start()

                aside(block, 2 * k, p).start()

    def handle_piece(k, p):
        handle(k, p)
        if p == PIECES - 1:
            handle(k, PIECES)

    def score_step(n, carry):
        k, j = (n + 2) // 4, (n + 2) % 4
        minor, other = j // 2, j % 2
        sign = (1 - 2 * minor) * (1 - 2 * other)
        block = 2 * ((y - sign * k * step_dir + 4 * ny) % ny) + core + other * step_dir

        @pl.when(n == 2)
        def _():
            for p in range(PIECES):
                handle_piece(1, p)

        if last_major > 1:
            t = n - 3
            for p in range(PIECES):

                @pl.when((n >= 3) & (n < 3 + 4 * (last_major - 1)) & (t % 4 == p))
                def _():
                    handle_piece(t // 4 + 2, p)

        @pl.when(other == 1)
        def _():
            for p in range(PIECES + 1):
                aside(block, n // 2, p).wait_recv()

        queries = blocks[pl.ds(PIECES * block, PIECES)].reshape(slots, width)
        wanted = members[block]
        inner = mm(held[...], queries, NT)
        kept = []
        for g in range(groups):
            lanes = slice(g * lane_group, (g + 1) * lane_group)
            value = inner[:, lanes] * scale_col[:, :lane_group]
            value = jnp.where(cluster_col[:, :lane_group] == wanted[:, lanes], value, LOWEST)
            kept.append(jnp.max(value.reshape(res_rows // 8, 8, lane_group), axis=0))
        best = kept[0] if groups == 1 else jnp.concatenate(kept, axis=1)
        best_own[block] = jnp.max(jnp.maximum(best, LOWEST), axis=0, keepdims=True)

        @pl.when(n == 0)
        def _():
            best_got[me_s] = best_own[me_s]

        @pl.when(n > 0)
        def _():
            remote(
                best_own.at[block],
                best_got.at[me_s],
                sems.at[BEST, 0],
                sems.at[BEST, 1],
                me_o,
                block,
            ).start()

        @pl.when(n == 1)
        def _():
            x = blocks[pl.ds(PIECES * me_s, PIECES)].reshape(slots, width)
            f = x.astype(F32)
            scale = lax.rsqrt(column_to_row(jnp.sum(f * f, axis=1, keepdims=True)) + EPS)
            mask = jnp.broadcast_to(members[me_s], (clusters, slots)) == (
                iota((clusters, slots), 0) + 1
            ).astype(F32)
            both = held_sums[...] + mm(split_weights(mask, scale), x)
            partial = both[:clusters] + both[clusters:]
            for s in range(splits):
                row, lane = s // chunks_in_row, (s % chunks_in_row) * chunk
                part[s] = partial[row : row + 1, lane : lane + chunk]

            @pl.loop(1, splits)
            def _(i):
                s = other_split(i)
                remote(
                    part.at[s], part_got.at[me_s], sems.at[PART, 0], sems.at[PART, 1], me_o, s
                ).start()

            part_got[me_s] = part[me_s]

        @pl.when(n == min(9, splits - 1))
        def _():
            wait_all(part_got, splits - 1, PART, 1)
            total_own[...] = jnp.sum(part_got[...], axis=0)

            @pl.loop(1, splits)
            def _(i):
                remote(
                    total_own,
                    total.at[me_s],
                    sems.at[TOTAL, 0],
                    sems.at[TOTAL, 1],
                    me_o,
                    other_split(i),
                ).start()

            total[me_s] = total_own[...]

        return carry

    lax.fori_loop(0, splits, score_step, 0)

    wait_all(best_got, splits - 1, BEST, 1)
    best = jnp.max(best_got[...], axis=0)
    for g in range(groups):
        ret_own[g] = best[:, g * lane_group : (g + 1) * lane_group]
    for r in range(owners - 1, 0, -1):
        remote(
            ret_own.at[r // owners_in_group],
            ret_got.at[r],
            sems.at[RET, 0],
            sems.at[RET, 1],
            source_of(r),
            me_s,
        ).start()
    ret_got[0] = ret_own[0]

    wait_all(total, splits - 1, TOTAL, 1)
    for j in range(clusters):
        bits = [total[j * chunks_in_row + i] for i in range(chunks_in_row)]
        v = bits[0] if chunks_in_row == 1 else jnp.concatenate(bits, axis=1)
        cent_ref[j : j + 1] = v * lax.rsqrt(jnp.sum(v * v, axis=1, keepdims=True) + EPS)

    wait_all(send_rows, owners - 1, ROWS, 0)
    wait_all(send_members, owners - 1, MEMBERS, 0)
    wait_all(part, splits - 1, PART, 0)
    wait_all(total, splits - 1, TOTAL, 0)
    wait_all(best_own, splits - 1, BEST, 0)
    for p in range(PIECES + 1):
        for k in range(1, last_major + 1):
            up(me_s, k, p).wait_send()
        for k in range(1, last_minor + 1):
            down(me_s, k, p).wait_send()
        for i in range(ny):
            aside(me_s, i, p).wait_send()

    wait_all(ret_got, owners - 1, RET, 1)
    lane_owner = lax.div(iota((owners, lane_group), 1), cap)
    mine = lane_owner == lax.rem(iota((owners, lane_group), 0), owners_in_group)
    value = jnp.concatenate([ret_got[r] for r in range(owners)], axis=0)
    value = jnp.where(mine, value, 0.0)
    high = value.astype(BF16).astype(F32)
    mid = (value - high).astype(BF16).astype(F32)
    low = value - high - mid
    picked = mm(jnp.concatenate([high, mid, low], axis=0).astype(BF16), place_hot)
    picked = picked[:owners] + picked[owners : 2 * owners] + picked[2 * owners :]
    max_ref[...] = own_scale * jnp.sum(target_hot * picked, axis=0, keepdims=True)
    wait_all(ret_got, owners - 1, RET, 0)


def body(new_rows, cluster_ids, slot_of_cluster, row_counts, resident):
    owners, splits = lax.axis_size("owner"), lax.axis_size("split")
    local, width = new_rows.shape
    clusters = row_counts.shape[2]
    res_rows = resident.shape[2]
    cap = 2 * local // owners
    slots = owners * cap
    lane_group = min(128, slots)
    chunk = clusters * width // splits
    ny = splits // 2
    vmem = pl.BlockSpec(memory_space=pltpu.VMEM)
    hbm = pl.BlockSpec(memory_space=pltpu.HBM)
    dma = pltpu.SemaphoreType.DMA
    major, minor = max(1, ny // 2), max(1, ny // 2 - 1)
    pieces = PIECES + 1
    best, centroids = pl.pallas_call(
        functools.partial(kernel, (owners, splits, local, width, clusters, res_rows, cap)),
        out_shape=(
            jax.ShapeDtypeStruct((1, local), F32),
            jax.ShapeDtypeStruct((clusters, width), F32),
        ),
        in_specs=[hbm] * 5,
        out_specs=(vmem, vmem),
        scratch_shapes=[
            pltpu.VMEM((1, local), I32),
            pltpu.VMEM((1, slot_of_cluster.shape[0]), I32),
            pltpu.SMEM((1, clusters), I32),
            pltpu.VMEM((local, width), BF16),
            pltpu.VMEM((res_rows, width), BF16),
            pltpu.VMEM((res_rows, 128), F32),
            pltpu.VMEM((res_rows, 128), F32),
            pltpu.VMEM((owners, cap, width), BF16),
            pltpu.VMEM((owners, 1, lane_group), F32),
            pltpu.VMEM((owners, cap, width), BF16),
            pltpu.VMEM((owners, 1, lane_group), F32),
            pltpu.VMEM((PIECES * splits, slots // PIECES, width), BF16),
            pltpu.VMEM((splits, 1, slots), F32),
            pltpu.VMEM((2 * clusters, width), F32),
            pltpu.VMEM((splits, 1, chunk), F32),
            pltpu.VMEM((splits, 1, chunk), F32),
            pltpu.VMEM((1, chunk), F32),
            pltpu.VMEM((splits, 1, chunk), F32),
            pltpu.VMEM((splits, 1, slots), F32),
            pltpu.VMEM((splits, 1, slots), F32),
            pltpu.VMEM((slots // lane_group, 1, lane_group), F32),
            pltpu.VMEM((owners, 1, lane_group), F32),
            dma((5,)),
            dma((PIECES,)),
            dma((6, 2)),
            dma((major, pieces)),
            dma((major, pieces)),
            dma((minor, pieces)),
            dma((minor, pieces)),
            dma((ny, pieces)),
            dma((ny, pieces)),
        ],
        compiler_params=pltpu.CompilerParams(
            collective_id=0, has_side_effects=True, vmem_limit_bytes=60 * 1024 * 1024
        ),
        cost_estimate=pl.CostEstimate(
            flops=2 * splits * slots * res_rows * width, bytes_accessed=4 << 20, transcendentals=0
        ),
    )(
        cluster_ids.reshape(1, -1),
        slot_of_cluster.reshape(1, -1),
        row_counts.reshape(1, -1),
        new_rows,
        resident.reshape(res_rows, width),
    )
    return best.reshape(-1), centroids


def solution(mesh):
    placed = (
        P(("owner", "split"), None),
        P(("owner", "split")),
        P(),
        P("owner", "split", None),
        P("owner", "split", None, None),
    )
    return jax.shard_map(
        body,
        mesh=mesh,
        in_specs=placed,
        out_specs=(P(("owner", "split")), P("owner", None)),
        check_vma=False,
    )
```

time: 61.4 us -> 54.5 us (0.89)
  Pallas kernels: 56.6 us -> 51.2 us
  local copies, waits for them, and re-layouts: 3.85 us -> 2.47 us
    pallas_call x1, Pallas kernels: 56.6 us -> 51.2 us  [body(): pl.pallas_call(functools.partial(kernel, (owners, splits, local, width, c...]
    unnamed x12 -> x4, local copies, waits for them, and re-layouts: 3.85 us -> 2.47 us
where the time goes in v2:
time: 54.5 us; the launch traced here: 54.4 us
  Pallas kernels  51.2 us (94%)
  local copies, waits for them, and re-layouts  2.47 us (5%)
  between operations  0.65 us (1%)
    pallas_call x1, Pallas kernels, body(): pl.pallas_call(functools.partial(kernel, (owners, splits, local, width, c...  51.2 us
    unnamed x4, local copies, waits for them, and re-layouts  2.47 us

profile of v2, /device:TPU:1, one launch (start us, length us, event | category | flops | bytes accessed | tf_op | source)
XLA Modules:
  0.0 54.4 jit_solution(8353180351505387627)
XLA Ops:
  0.6 51.2 %shard_map.68 = (f32[1,128]{1,0:T(1,128)}, f32[8,256]{1,0:T(8,128)}) custom-call(s32[1,128]{1,0:T(1,128)} %bitcast.7, s32[1,256]{1,0:T(1,128)} %bitcast.6, s32[1,8]{1,0:T(1,128)} %bitcast.8, bf16[128,256]{1,0:T(8,128)(2,1)} %rows_hbm.1, bf16[2048,256]{1,0:T(8,128)(2,1)} %bitcast.5), custom_call_target="tpu_custom_call" | custom-call | flops 4294967296 | bytes 4194304 | tf_op jit(solution)/shard_map/pallas_call | solution.py:517
  51.9 0.0 copy-start
  51.9 0.7 %copy-done = f32[1,128]{1,0:T(1,128)S(1)} copy-done((f32[1,128]{1,0:T(1,128)S(1)}, f32[1,128]{1,0:T(1,128)}, u32[]{:S(2)}) %copy-start) | copy-done | bytes 536
  52.5 0.5 copy.9
  53.1 1.3 %copy.10 = f32[8,256]{1,0:T(8,128)} copy(f32[8,256]{1,0:T(8,128)} %get-tuple-element.9) | data formatting | bytes 16384
Async XLA Ops:
  51.9 0.7 %copy-start = (f32[1,128]{1,0:T(1,128)S(1)}, f32[1,128]{1,0:T(1,128)}, u32[]{:S(2)}) copy-start(f32[1,128]{1,0:T(1,128)} %get-tuple-element.4) | copy-start | bytes 1540

commit v3 on v2

--- a/solution.py
+++ b/solution.py
@@ -556,17 +556,22 @@
             dma((ny, pieces)),
         ],
         compiler_params=pltpu.CompilerParams(
-            collective_id=0, has_side_effects=True, vmem_limit_bytes=60 * 1024 * 1024
+            collective_id=0, has_side_effects=True, vmem_limit_bytes=48 * 1024 * 1024
         ),
         cost_estimate=pl.CostEstimate(
             flops=2 * splits * slots * res_rows * width, bytes_accessed=4 << 20, transcendentals=0
         ),
     )(
-        cluster_ids.reshape(1, -1),
-        slot_of_cluster.reshape(1, -1),
-        row_counts.reshape(1, -1),
-        new_rows,
-        resident.reshape(res_rows, width),
+        *(
+            pltpu.with_memory_space_constraint(x, pltpu.HBM)
+            for x in (
+                cluster_ids.reshape(1, -1),
+                slot_of_cluster.reshape(1, -1),
+                row_counts.reshape(1, -1),
+                new_rows,
+                resident.reshape(res_rows, width),
+            )
+        )
     )
     return best.reshape(-1), centroids
 

time: 54.5 us -> 52.5 us (0.963)
  local copies, waits for them, and re-layouts: 2.47 us -> 1.11 us
  Pallas kernels: 51.2 us -> 50.6 us
    unnamed x4 -> x2, local copies, waits for them, and re-layouts: 2.47 us -> 1.11 us
    pallas_call x1, Pallas kernels: 51.2 us -> 50.6 us  [body(): pl.pallas_call(functools.partial(kernel, (owners, splits, local, width, c...]
where the time goes in v3:
time: 52.5 us; the launch traced here: 52.4 us
  Pallas kernels  50.6 us (96%)
  local copies, waits for them, and re-layouts  1.11 us (2%)
  between operations  0.64 us (1%)
    pallas_call x1, Pallas kernels, body(): pl.pallas_call(functools.partial(kernel, (owners, splits, local, width, c...  50.6 us
    unnamed x2, local copies, waits for them, and re-layouts  1.11 us

profile of v3, /device:TPU:1, one launch (start us, length us, event | category | flops | bytes accessed | tf_op | source)
XLA Modules:
  0.0 52.4 jit_solution(384265690743524739)
XLA Ops:
  0.6 50.6 %shard_map.68 = (f32[1,128]{1,0:T(1,128)S(1)}, f32[8,256]{1,0:T(8,128)S(1)}) custom-call(s32[1,128]{1,0:T(1,128)} %bitcast.8, s32[1,256]{1,0:T(1,128)} %bitcast.7, s32[1,8]{1,0:T(1,128)} %bitcast.9, bf16[128,256]{1,0:T(8,128)(2,1)} %rows_hbm.1, bf16[2048,256]{1,0:T(8,128)(2,1)} %bitcast.6), custom_call_target="tpu_custom_call" | custom-call | flops 4294967296 | bytes 4194304 | tf_op jit(solution)/shard_map/pallas_call | solution.py:517
  51.3 0.5 copy.9
  51.8 0.6 %copy.10 = f32[8,256]{1,0:T(8,128)} copy(f32[8,256]{1,0:T(8,128)S(1)} %get-tuple-element.9) | data formatting | bytes 16384

commit v4 on v3

--- a/solution.py
+++ b/solution.py
@@ -269,11 +269,13 @@
     )
 
     def piece_of(block, p):
-        return members.at[block] if p == PIECES else blocks.at[PIECES * block + p]
-
-    def up(block, k, p, hops=1):
+        if isinstance(p, int) and p == PIECES:
+            return members.at[block]
+        return blocks.at[PIECES * block + p]
+
+    def up(block, k, p):
         ref = piece_of(block, p)
-        return remote(ref, ref, major_send.at[k - 1, p], major_recv.at[k - 1, p], me_o, at_y(hops))
+        return remote(ref, ref, major_send.at[k - 1, p], major_recv.at[k - 1, p], me_o, at_y(1))
 
     def down(block, k, p):
         ref = piece_of(block, p)
@@ -282,11 +284,6 @@
     def aside(block, index, p):
         ref = piece_of(block, p)
         return remote(ref, ref, sib_send.at[index, p], sib_recv.at[index, p], me_o, sibling)
-
-    skip = ny == 8
-
-    def skipped(p):
-        return skip and p >= PIECES - 1
 
     def start_own(p):
         up(me_s, 1, p).start()
@@ -320,65 +317,17 @@
     def handle(k, p):
         block = at_y(-k)
         up(block, k, p).wait_recv()
-        if not skipped(p):
-
-            @pl.when(k < last_major)
-            def _():
-                up(block, k + 1, p).start()
-
-        else:
-
-            @pl.when(k < 3)
-            def _():
-                up(block, k + 1, p).start()
-
-            @pl.when(k == 2)
-            def _():
-                up(block, 4, p, hops=2).start()
-
+        if k < last_major:
+            up(block, k + 1, p).start()
         aside(block, 2 * k - 1, p).start()
-        if last_minor:
-
-            @pl.when(k <= last_minor)
-            def _():
-                block = at_y(k)
-                down(block, k, p).wait_recv()
-
-                @pl.when(k < last_minor)
-                def _():
-                    down(block, k + 1, p).start()
-
-                aside(block, 2 * k, p).start()
-
-    def handle_piece(k, p):
-        handle(k, p)
-        if p == PIECES - 1:
-            handle(k, PIECES)
-
-    def score_step(n, carry):
-        k, j = (n + 2) // 4, (n + 2) % 4
-        minor, other = j // 2, j % 2
-        sign = (1 - 2 * minor) * (1 - 2 * other)
-        block = 2 * ((y - sign * k * step_dir + 4 * ny) % ny) + core + other * step_dir
-
-        @pl.when(n == 2)
-        def _():
-            for p in range(PIECES):
-                handle_piece(1, p)
-
-        if last_major > 1:
-            t = n - 3
-            for p in range(PIECES):
-
-                @pl.when((n >= 3) & (n < 3 + 4 * (last_major - 1)) & (t % 4 == p))
-                def _():
-                    handle_piece(t // 4 + 2, p)
-
-        @pl.when(other == 1)
-        def _():
-            for p in range(PIECES + 1):
-                aside(block, n // 2, p).wait_recv()
-
+        if k <= last_minor:
+            block = at_y(k)
+            down(block, k, p).wait_recv()
+            if k < last_minor:
+                down(block, k + 1, p).start()
+            aside(block, 2 * k, p).start()
+
+    def score(block):
         queries = blocks[pl.ds(PIECES * block, PIECES)].reshape(slots, width)
         wanted = members[block]
         inner = mm(held[...], queries, NT)
@@ -391,65 +340,90 @@
         best = kept[0] if groups == 1 else jnp.concatenate(kept, axis=1)
         best_own[block] = jnp.max(jnp.maximum(best, LOWEST), axis=0, keepdims=True)
 
-        @pl.when(n == 0)
-        def _():
+    def send_best(block):
+        remote(
+            best_own.at[block],
+            best_got.at[me_s],
+            sems.at[BEST, 0],
+            sems.at[BEST, 1],
+            me_o,
+            block,
+        ).start()
+
+    def new_sums():
+        x = blocks[pl.ds(PIECES * me_s, PIECES)].reshape(slots, width)
+        f = x.astype(F32)
+        scale = lax.rsqrt(column_to_row(jnp.sum(f * f, axis=1, keepdims=True)) + EPS)
+        mask = jnp.broadcast_to(members[me_s], (clusters, slots)) == (
+            iota((clusters, slots), 0) + 1
+        ).astype(F32)
+        both = held_sums[...] + mm(split_weights(mask, scale), x)
+        partial = both[:clusters] + both[clusters:]
+        for s in range(splits):
+            row, lane = s // chunks_in_row, (s % chunks_in_row) * chunk
+            part[s] = partial[row : row + 1, lane : lane + chunk]
+
+        @pl.loop(1, splits)
+        def _(i):
+            s = other_split(i)
+            remote(
+                part.at[s], part_got.at[me_s], sems.at[PART, 0], sems.at[PART, 1], me_o, s
+            ).start()
+
+        part_got[me_s] = part[me_s]
+
+    def share_totals():
+        wait_all(part_got, splits - 1, PART, 1)
+        total_own[...] = jnp.sum(part_got[...], axis=0)
+
+        @pl.loop(1, splits)
+        def _(i):
+            remote(
+                total_own,
+                total.at[me_s],
+                sems.at[TOTAL, 0],
+                sems.at[TOTAL, 1],
+                me_o,
+                other_split(i),
+            ).start()
+
+        total[me_s] = total_own[...]
+
+    for k in range(last_major + 1):
+
+        @pl.loop(0, 2 if k in (0, last_major) else 4)
+        def _(j):
+            minor, other = j // 2, j % 2
+            sign = (1 - 2 * minor) * (1 - 2 * other)
+            block = 2 * ((y - sign * k * step_dir + 4 * ny) % ny) + core + other * step_dir
+            index = max(2 * k - 1, 0) + minor
+
+            @pl.when(other == 1)
+            def _():
+                for p in range(PIECES + 1):
+                    aside(block, index, p).wait_recv()
+
+            score(block)
+            if k == 0:
+
+                @pl.when(j == 1)
+                def _():
+                    send_best(block)
+
+            else:
+                send_best(block)
+            if 0 < k < last_major:
+                handle(k + 1, j)
+
+        if k == 0:
             best_got[me_s] = best_own[me_s]
-
-        @pl.when(n > 0)
-        def _():
-            remote(
-                best_own.at[block],
-                best_got.at[me_s],
-                sems.at[BEST, 0],
-                sems.at[BEST, 1],
-                me_o,
-                block,
-            ).start()
-
-        @pl.when(n == 1)
-        def _():
-            x = blocks[pl.ds(PIECES * me_s, PIECES)].reshape(slots, width)
-            f = x.astype(F32)
-            scale = lax.rsqrt(column_to_row(jnp.sum(f * f, axis=1, keepdims=True)) + EPS)
-            mask = jnp.broadcast_to(members[me_s], (clusters, slots)) == (
-                iota((clusters, slots), 0) + 1
-            ).astype(F32)
-            both = held_sums[...] + mm(split_weights(mask, scale), x)
-            partial = both[:clusters] + both[clusters:]
-            for s in range(splits):
-                row, lane = s // chunks_in_row, (s % chunks_in_row) * chunk
-                part[s] = partial[row : row + 1, lane : lane + chunk]
-
-            @pl.loop(1, splits)
-            def _(i):
-                s = other_split(i)
-                remote(
-                    part.at[s], part_got.at[me_s], sems.at[PART, 0], sems.at[PART, 1], me_o, s
-                ).start()
-
-            part_got[me_s] = part[me_s]
-
-        @pl.when(n == min(9, splits - 1))
-        def _():
-            wait_all(part_got, splits - 1, PART, 1)
-            total_own[...] = jnp.sum(part_got[...], axis=0)
-
-            @pl.loop(1, splits)
-            def _(i):
-                remote(
-                    total_own,
-                    total.at[me_s],
-                    sems.at[TOTAL, 0],
-                    sems.at[TOTAL, 1],
-                    me_o,
-                    other_split(i),
-                ).start()
-
-            total[me_s] = total_own[...]
-
-        return carry
-
-    lax.fori_loop(0, splits, score_step, 0)
+            new_sums()
+            for p in range(PIECES):
+                handle(1, p)
+        if k < last_major:
+            handle(k + 1, PIECES)
+        if k == last_minor:
+            share_totals()
 
     wait_all(best_got, splits - 1, BEST, 1)
     best = jnp.max(best_got[...], axis=0)

time: 52.5 us -> 52.3 us (level)
  no operation moved by 1% of the time
where the time goes in v4:
time: 52.3 us; the launch traced here: 52.1 us
  Pallas kernels  50.4 us (96%)
  local copies, waits for them, and re-layouts  1.11 us (2%)
  between operations  0.64 us (1%)
    pallas_call x1, Pallas kernels, body(): pl.pallas_call(functools.partial(kernel, (owners, splits, local, width, c...  50.4 us
    unnamed x2, local copies, waits for them, and re-layouts  1.11 us

profile of v4, /device:TPU:1, one launch (start us, length us, event | category | flops | bytes accessed | tf_op | source)
XLA Modules:
  0.0 52.1 jit_solution(9235087679899999756)
XLA Ops:
  0.6 50.4 %shard_map.68 = (f32[1,128]{1,0:T(1,128)S(1)}, f32[8,256]{1,0:T(8,128)S(1)}) custom-call(s32[1,128]{1,0:T(1,128)} %bitcast.8, s32[1,256]{1,0:T(1,128)} %bitcast.7, s32[1,8]{1,0:T(1,128)} %bitcast.9, bf16[128,256]{1,0:T(8,128)(2,1)} %rows_hbm.1, bf16[2048,256]{1,0:T(8,128)(2,1)} %bitcast.6), custom_call_target="tpu_custom_call" | custom-call | flops 4294967296 | bytes 4194304 | tf_op jit(solution)/shard_map/pallas_call | solution.py:491
  51.0 0.5 copy.9
  51.5 0.6 %copy.10 = f32[8,256]{1,0:T(8,128)} copy(f32[8,256]{1,0:T(8,128)S(1)} %get-tuple-element.9) | data formatting | bytes 16384

commit v5 on v4

--- a/solution.py
+++ b/solution.py
@@ -422,7 +422,7 @@
                 handle(1, p)
         if k < last_major:
             handle(k + 1, PIECES)
-        if k == last_minor:
+        if k == last_major:
             share_totals()
 
     wait_all(best_got, splits - 1, BEST, 1)

time: 52.3 us -> 52.2 us (level)
  no operation moved by 1% of the time
where the time goes in v5:
time: 52.2 us; the launch traced here: 52.1 us
  Pallas kernels  50.3 us (96%)
  local copies, waits for them, and re-layouts  1.11 us (2%)
  between operations  0.64 us (1%)
    pallas_call x1, Pallas kernels, body(): pl.pallas_call(functools.partial(kernel, (owners, splits, local, width, c...  50.3 us
    unnamed x2, local copies, waits for them, and re-layouts  1.11 us

profile of v5, /device:TPU:1, one launch (start us, length us, event | category | flops | bytes accessed | tf_op | source)
XLA Modules:
  0.0 52.1 jit_solution(5653620430474823321)
XLA Ops:
  0.6 50.3 %shard_map.68 = (f32[1,128]{1,0:T(1,128)S(1)}, f32[8,256]{1,0:T(8,128)S(1)}) custom-call(s32[1,128]{1,0:T(1,128)} %bitcast.8, s32[1,256]{1,0:T(1,128)} %bitcast.7, s32[1,8]{1,0:T(1,128)} %bitcast.9, bf16[128,256]{1,0:T(8,128)(2,1)} %rows_hbm.1, bf16[2048,256]{1,0:T(8,128)(2,1)} %bitcast.6), custom_call_target="tpu_custom_call" | custom-call | flops 4294967296 | bytes 4194304 | tf_op jit(solution)/shard_map/pallas_call | solution.py:491
  51.0 0.5 copy.9
  51.5 0.6 %copy.10 = f32[8,256]{1,0:T(8,128)} copy(f32[8,256]{1,0:T(8,128)S(1)} %get-tuple-element.9) | data formatting | bytes 16384
